TPU v7x, 32 devices: a whole 2x2x4 slice. The times are simulated.
32 devices in a mesh: terms: 8 (over y, x, core), rows: 4 (over z).
Axes of the slice: x: 2, y: 2, z: 4, core: 2. Of those that a mesh axis runs over, the one named last changes fastest.
Arguments:
- psi: float32 [2, 768, 768], P(None, 'rows'), may hold values from -6 to 6
- left_ops: float32 [8, 768, 768], P('terms', 'rows'), may hold values from -0.21875 to 0.21875
- right_ops: float32 [16, 768, 768], P('terms', 'rows'), may hold values from -0.09375 to 0.09375
- term_count: int32 [8], P('terms'), may hold values from 1 to 3, 12 in all
- right_slot: int32 [24], P('terms'), may hold values from 0 to 1
- sector: int32 [24], P('terms'), may hold values from 0 to 1
- sign_bit: int32 [24], P('terms'), may hold values from 0 to 1
Outputs:
- sigma: float32 [2, 768, 768], P(None, 'rows', 'terms')
Inputs may be any that keep to these rules, and one draw needn't show every extreme that they name: Owner o's live terms are its first term_count[o] slots of 3; right_slot, sector and sign_bit of the other slots have no effect.
All inputs are finite; a program needn't handle non-finite values. No bound on the sum of `term_count` on one device may be relied on, other than what follows from the above.
Results may differ from a plain program's by a relative error of at most 0.0003.
Values sent between devices are 32-bit elements; how exact they have to be, the bound alone decides.
A program may use at most 64 MiB of HBM per device.

v0:
```python
import jax
import jax.numpy as jnp
from jax import lax
from jax.sharding import PartitionSpec as P

highest_mode = lax.Precision.HIGHEST


def passed_along(block, axis, distance):
    devices = range(lax.axis_size(axis))
    route = [((i - distance) % len(devices), i) for i in devices]
    return lax.ppermute(block, axis, route)


def per_device(psi, left_ops, right_ops, term_count, right_slot, sector, sign_bit):
    slot_count = right_slot.shape[0]
    sector_count = psi.shape[0]
    live_count = term_count[0]
    is_live = lax.iota(jnp.int32, slot_count) < live_count
    term_weight = jnp.where(is_live, 2.0 * sign_bit.astype(jnp.float32) - 1.0, 0.0)
    left_rows = left_ops[0]
    inner_rows = jnp.einsum(
        "an,snb->sab",
        left_rows,
        lax.all_gather(psi, "rows", axis=1, tiled=True),
        precision=highest_mode,
    )
    half_axis = lax.axis_size("terms") // 2
    moved_right = passed_along(right_ops, "terms", half_axis)
    segment = lax.all_gather(moved_right, "rows", axis=1, tiled=True)
    summed_zero = jnp.zeros((sector_count, inner_rows.shape[1], segment.shape[1]), jnp.float32)

    def one_term(index, summed):
        right_block = lax.dynamic_index_in_dim(segment, right_slot[index], 0, keepdims=False)
        source = lax.dynamic_index_in_dim(inner_rows, sector[index], 0, keepdims=False)
        product = term_weight[index] * lax.dot_general(
            source, right_block, (((1,), (1,)), ((), ())), precision=highest_mode
        )
        return summed.at[sector[index]].add(product)

    partial_value = lax.fori_loop(0, live_count, one_term, summed_zero)
    return lax.psum_scatter(partial_value, "terms", scatter_dimension=2, tiled=True)


def solution(mesh):
    return jax.shard_map(
        per_device,
        mesh=mesh,
        in_specs=(
            P(None, "rows", None),
            P("terms", "rows", None),
            P("terms", "rows", None),
            P("terms"),
            P("terms"),
            P("terms"),
            P("terms"),
        ),
        out_specs=P(None, "rows", "terms"),
        check_vma=False,
    )
```

profile of v0, /device:TPU:25, one launch (start us, length us, event | category | flops | bytes accessed | tf_op | source)
XLA Modules:
  0.0 273.2 jit_solution(2857333216381697852)
XLA Ops:
  6.5 0.0 copy-start
  6.5 0.0 copy-start.3
  6.5 0.0 copy-start.4
  6.5 0.0 all-gather.3.cloned.1.call-start
  6.5 0.7 all-gather.3.cloned.1.call-update
  7.3 0.0 all-gather.5.cloned.1.call-start
  7.3 0.6 copy-done.3
  7.9 1.2 collective-permute-start
  9.1 25.7 %collective-permute-done = f32[2,192,768]{2,1,0:T(8,128)S(1)} collective-permute-done((f32[2,192,768]{2,1,0:T(8,128)S(1)}, f32[2,192,768]{2,1,0:T(8,128)S(1)}, u32[]{:S(2)}, u32[]{:S(2)}) %collective-permute-start) | collective-permute-done | bytes 1179680 | tf_op jit(solution)/shard_map/ppermute | solution.py:12
  34.8 0.0 copy-start.1
  34.8 1.0 copy-done.1
  35.8 0.0 all-gather.5.cloned.1.call-update
  35.9 0.0 reduce-scatter.4.cloned.1.call-start
  36.6 0.0 copy-done.4
  36.6 60.2 %all-gather.3.cloned.1.call-done = f32[2,768,768]{2,1,0:T(8,128)} async-done(((f32[2,192,768]{2,1,0:T(8,128)}), f32[2,768,768]{2,1,0:T(8,128)}) %all-gather.3.cloned.1.call-update) | async-done | bytes 4718608 | tf_op jit(solution)/shard_map/all_gather | solution.py:25
  96.8 0.0 copy-done
  96.8 5.5 %convolution_bitcast_fusion = f32[2,192,768]{2,1,0:T(8,128)S(1)} fusion(f32[2,768,768]{2,1,0:T(8,128)} %all-gather.3.cloned.1.call-done, f32[1,192,768]{2,1,0:T(8,128)S(1)} %copy-done), kind=kOutput, calls=%fused_computation.12 | convolution fusion | flops 2717908992 | bytes 6488064 | tf_op jit(solution)/shard_map/an,snb->sab/dot_general | solution.py:22
  102.3 0.0 copy-start.2
  102.3 0.0 copy-start.5
  102.3 0.0 copy-start.6
  102.4 83.9 %all-gather.5.cloned.1.call-done = f32[2,768,768]{2,1,0:T(8,128)} async-done(((f32[2,192,768]{2,1,0:T(8,128)}), f32[2,768,768]{2,1,0:T(8,128)}) %all-gather.5.cloned.1.call-update) | async-done | bytes 4718608 | tf_op jit(solution)/shard_map/all_gather | solution.py:30
  186.2 0.1 broadcast_in_dim.8
  186.3 0.0 copy-done.2
  186.3 0.0 copy-done.5
  186.3 0.0 copy-done.6
  186.3 13.2 %while.11 = (s32[]{:T(128)}, f32[2,192,768]{2,1,0:T(8,128)S(1)}, s32[]{:T(128)}, s32[3]{0:T(128)S(1)}, f32[3]{0:T(128)S(1)}, /*index=5*/f32[2,192,768]{2,1,0:T(8...) while((s32[]{:T(128)}, f32[2,192,768]{2,1,0:T(8,128)S(1)}, ...), condition=%wide.region_2.3_spmd, body=%wide.region_0.2_spmd.sunk | while | flops 1359396864 | bytes 4131120 | solution.py:41
  187.0 0.6 dynamic_slice.43
  189.5 0.6 dynamic_slice.45
  190.1 0.6 dynamic_slice.44
  192.7 0.8 and_reduce_fusion.2
  193.5 5.4 %fusion.28 = f32[2,192,768]{2,1,0:T(8,128)S(1)} fusion(f32[2,192,768]{2,1,0:T(8,128)S(1)} %get-tuple-element.142, s32[]{:T(128)} %select_n.27, f32[2,768,768]{2,1,0:T(8,128)} %get-tuple-element.162, s32[]{:T(128)S(6)} %select_n.28, f32[2,192,768]{2,1,0:T(8,128)S(1)} %get-tuple-element.160, f32[]{:T(128)} %bitcast.50, pred[]{:T(512)} %and_reduce_fusion.2), kind=kOutput, calls=%fused_computation.7.clone.1 | convolution fusion | flops 1359396864 | bytes 4130820 | tf_op jit(solution)/shard_map/while/body/dot_general | solution.py:36
  199.6 0.8 copy.8
  200.4 2.3 reshape.35
  202.7 0.0 reduce-scatter.4.cloned.1.call-update
  202.7 62.1 %reduce-scatter.4.cloned.1.call-done = f32[96,384]{1,0:T(8,128)} async-done(((f32[768,384]{1,0:T(8,128)}), f32[96,384]{1,0:T(8,128)}) %reduce-scatter.4.cloned.1.call-update) | async-done | bytes 147472
  264.8 1.1 reshape.36
  265.9 0.8 copy.9
  (1 shorter events, 0.0 us)
Async XLA Ops:
  6.5 90.2 %copy-start = (f32[1,192,768]{2,1,0:T(8,128)S(1)}, f32[1,192,768]{2,1,0:T(8,128)}, u32[]{:S(2)}) copy-start(f32[1,192,768]{2,1,0:T(8,128)} %param.12) | copy-start | bytes 1769476
  6.5 1.3 copy-start.3
  6.5 30.0 %copy-start.4 = (s32[3]{0:T(128)S(1)}, s32[3]{0:T(128)}, u32[]{:S(2)}) copy-start(s32[3]{0:T(128)} %param.17) | copy-start | bytes 40
  6.5 90.2 %all-gather.3.cloned.1.call-start = ((), (), s32[]{:S(2)}) async-start(), calls=%async_computation.1 | async-start | bytes 5898240 | tf_op jit(solution)/shard_map/all_gather | solution.py:25
  7.3 179.0 %all-gather.5.cloned.1.call-start = ((), (), s32[]{:S(2)}) async-start(), calls=%async_computation.2 | async-start | bytes 5898240 | tf_op jit(solution)/shard_map/all_gather | solution.py:30
  7.9 26.9 %collective-permute-start = (f32[2,192,768]{2,1,0:T(8,128)S(1)}, f32[2,192,768]{2,1,0:T(8,128)S(1)}, u32[]{:S(2)}, u32[]{:S(2)}) collective-permute-start(f32[2,192,768]{2,1,0:T(8,128)S(1)} %copy-done.3), channel_id=1, source_target_pairs={{16,0},{20,4},{24,8},{28,12},{0,16},{4,20},{8,24},{12,28},{17,1},{... | collective-permute-start | bytes 3538952 | tf_op jit(solution)/shard_map/ppermute | solution.py:12
  34.8 1.0 copy-start.1
  35.9 228.9 %reduce-scatter.4.cloned.1.call-start = ((), (), s32[]{:S(2)}) async-start(), calls=%async_computation.3 | async-start | bytes 1327104
  102.3 84.0 %copy-start.2 = (s32[3]{0:T(128)S(1)}, s32[3]{0:T(128)}, u32[]{:S(2)}) copy-start(s32[3]{0:T(128)} %constant.43.clone.1) | copy-start | bytes 40
  102.3 84.0 %copy-start.5 = (s32[3]{0:T(128)S(1)}, s32[3]{0:T(128)}, u32[]{:S(2)}) copy-start(s32[3]{0:T(128)} %param.16) | copy-start | bytes 40
  102.3 84.0 %copy-start.6 = (s32[3]{0:T(128)S(1)}, s32[3]{0:T(128)}, u32[]{:S(2)}) copy-start(s32[3]{0:T(128)} %param.15) | copy-start | bytes 40
Sparse Core Ops, SparseCore 0:
  8.9 87.7 all-gather.2
  98.3 87.8 all-gather.4
  202.8 61.9 reduce-scatter.3
where the time goes:
time: 276 us; the launch traced here: 273 us
  waiting for transfers between devices  233 us (84%)
  between operations  13.9 us (5%)
  matrix products  11 us (4%)
  local copies, waits for them, and re-layouts  8.59 us (3%)
  loops' own time  5.13 us (2%)
    all_gather x1, waiting for transfers between devices, per_device(): segment = lax.all_gather(moved_right, 'rows', axis=1, tiled=True)  83.9 us
    unnamed x4, waiting for transfers between devices  62.8 us
    all_gather x1, waiting for transfers between devices, per_device(): lax.all_gather(psi, 'rows', axis=1, tiled=True)  60.2 us
    ppermute x1, waiting for transfers between devices, passed_along(): return lax.ppermute(block, axis, route)  25.7 us
    unnamed x18, local copies, waits for them, and re-layouts  6.64 us
    dot_general x1, matrix products, per_device(): jnp.einsum('an,snb->sab', left_rows, lax.all_gather(psi, 'rows', axis=1,...  5.54 us
  transfers between devices with their start and end apart: 4, of which 4 were waited for; matrix products, arithmetic and copies ran while one was open for 2% of the time, Pallas kernels for 0%

commit v1 on v0

v1 whole, which is shorter than its diff:
```python
import functools

import jax
import jax.numpy as jnp
from jax import lax
from jax.experimental import pallas as pl
from jax.experimental.pallas import tpu as pltpu
from jax.sharding import PartitionSpec as P

highest_mode = lax.Precision.HIGHEST
MESH = pl.DeviceIdType.MESH


def passed_along(block, axis, distance):
    devices = range(lax.axis_size(axis))
    route = [((i - distance) % len(devices), i) for i in devices]
    return lax.ppermute(block, axis, route)


def term_weights(right_slot, term_count, sign_bit):
    is_live = lax.iota(jnp.int32, right_slot.shape[0]) < term_count[0]
    return jnp.where(is_live, 2.0 * sign_bit.astype(jnp.float32) - 1.0, 0.0)


def plain_device(psi, left_ops, right_ops, term_count, right_slot, sector, sign_bit):
    live_count = term_count[0]
    term_weight = term_weights(right_slot, term_count, sign_bit)
    inner_rows = jnp.einsum(
        "an,snb->sab",
        left_ops[0],
        lax.all_gather(psi, "rows", axis=1, tiled=True),
        precision=highest_mode,
    )
    half_axis = lax.axis_size("terms") // 2
    moved_right = passed_along(right_ops, "terms", half_axis)
    segment = lax.all_gather(moved_right, "rows", axis=1, tiled=True)
    summed_zero = jnp.zeros((psi.shape[0], inner_rows.shape[1], segment.shape[1]), jnp.float32)

    def one_term(index, summed):
        right_block = lax.dynamic_index_in_dim(segment, right_slot[index], 0, keepdims=False)
        source = lax.dynamic_index_in_dim(inner_rows, sector[index], 0, keepdims=False)
        product = term_weight[index] * lax.dot_general(
            source, right_block, (((1,), (1,)), ((), ())), precision=highest_mode
        )
        return summed.at[sector[index]].add(product)

    partial_value = lax.fori_loop(0, live_count, one_term, summed_zero)
    return lax.psum_scatter(partial_value, "terms", scatter_dimension=2, tiled=True)


def split16(value):
    high = value.astype(jnp.bfloat16)
    low = (value - high.astype(jnp.float32)).astype(jnp.bfloat16)
    return high, low


def dot3(a, b, dims):
    (a_high, a_low), (b_high, b_low) = a, b
    dot = functools.partial(
        lax.dot_general,
        dimension_numbers=(dims, ((), ())),
        preferred_element_type=jnp.float32,
    )
    return dot(a_high, b_high) + (dot(a_high, b_low) + dot(a_low, b_high))


def kernel(
    T, Z, CH,
    psi_ref, left_ref, right_ref, mix_ref, out_ref,
    psi_all, left_all, mix_in, y_high, y_low, part, part_in, fin,
    c_high, c_low,
    mix_s, mix_r, pz_s, pz_r, pp_s, pp_r, ly_s, lz_s, l_r, sc_s, sc_r, fin_s, fin_r,
):
    S, rows, M = psi_ref.shape
    R = right_ref.shape[0]
    H = T // Z
    sub = rows // T
    width = rows // H
    lrows = rows // CH
    t = lax.axis_index("terms")
    z = lax.axis_index("rows")
    bit_k, bit_x = lax.rem(t, 2), lax.rem(t // 2, 2)
    tk = t + 1 - 2 * bit_k
    tx = t + 2 - 4 * bit_x
    ty = lax.rem(t + 4, T)
    txy = lax.rem(tx + 4, T)

    def near(i):
        n_near = jnp.minimum(z, Z - 1 - z)
        half = (i + 1) // 2
        paired = z - half if i % 2 else z + half
        rest = jnp.where(z < Z - 1 - z, i, Z - 1 - i)
        return jnp.where(i <= 2 * n_near, paired, rest)

    def remote(src, dst, send, recv, tt, zz):
        return pltpu.make_async_remote_copy(
            src_ref=src, dst_ref=dst, send_sem=send, recv_sem=recv,
            device_id=(tt, zz), device_id_type=MESH,
        )

    def rows_of(device):
        return pl.ds(pl.multiple_of(device * sub, 8), sub)

    barrier = pltpu.get_barrier_semaphore()
    for d in range(1, T):
        pl.semaphore_signal(barrier, 1, device_id=(lax.rem(t + d, T), z), device_id_type=MESH)
    for step in (-1, 1):
        inside = (z + step >= 0) & (z + step < Z)

        @pl.when(inside)
        def _():
            pl.semaphore_signal(barrier, 1, device_id=(t, z + step), device_id_type=MESH)

    source_plane = t // H
    own_final = source_plane == z
    for e in range(T):
        @pl.when(jnp.logical_not(own_final & (t == e)))
        def _():
            pl.semaphore_signal(barrier, 1, device_id=(jnp.int32(e), source_plane), device_id_type=MESH)

    greeted = 2 * T - 1 + jnp.where(z > 0, 1, 0) + jnp.where(z < Z - 1, 1, 0)
    pl.semaphore_wait(barrier, greeted - jnp.where(own_final, 1, 0))

    def psi_own(step):
        return remote(
            psi_ref.at[:, rows_of(t), :], psi_all.at[z, :, rows_of(t), :],
            pz_s.at[(step + 1) // 2, z], pz_r.at[z], t, z + step,
        )

    def psi_pass(zs, step):
        view = psi_all.at[zs, :, rows_of(t), :]
        return remote(view, view, pz_s.at[(step + 1) // 2, zs], pz_r.at[zs], t, z + step)

    def spread(zs, kind, piece, target):
        view = psi_all.at[zs, :, rows_of(piece), :]
        return remote(view, view, pp_s.at[zs, kind], pp_r.at[zs, kind], target, z)

    def spread_copies(zs):
        return [
            spread(zs, 0, t, ty), spread(zs, 1, t, tx), spread(zs, 2, ty, tx),
            spread(zs, 3, t, tk), spread(zs, 4, ty, tk), spread(zs, 5, tx, tk),
            spread(zs, 6, txy, tk),
        ]

    def left_first(c):
        part_rows = pl.ds(c * lrows, lrows)
        return remote(
            left_ref.at[part_rows, :], left_all.at[z, part_rows, :],
            ly_s.at[c], l_r.at[z, c], ty, z,
        )

    def left_pass(zs, c, step):
        view = left_all.at[zs, pl.ds(c * lrows, lrows), :]
        return remote(view, view, lz_s.at[(step + 1) // 2, zs, c], l_r.at[zs, c], t, z + step)

    def can_pass(zs, step):
        if step == 1:
            return (zs <= z) & (z < Z - 1)
        return (zs >= z) & (z > 0)

    def scatter(zs, d):
        peer = lax.rem(t + d, T)
        return remote(
            part.at[zs, rows_of(peer), :], part_in.at[zs, d - 1],
            sc_s.at[zs, d - 1], sc_r.at[zs, d - 1], peer, z,
        )

    def final(zs, h):
        return remote(
            fin.at[zs, h], out_ref.at[:, rows_of(t), :],
            fin_s.at[zs, h], fin_r.at[t], z * H + h, zs,
        )

    def fill_y(zs, source, s):
        value = dot3(split16(source), (c_high[s], c_low[s]), ((1,), (1,)))
        high, low = split16(value)
        y_high[s, pl.ds(pl.multiple_of(zs * rows, 16), rows), :] = high
        y_low[s, pl.ds(pl.multiple_of(zs * rows, 16), rows), :] = low

    def left_arrives(zs):
        for c in range(CH):
            left_pass(zs, c, 1).wait_recv()
            for step in (-1, 1):
                @pl.when(can_pass(zs, step))
                def _():
                    left_pass(zs, c, step).start()

    def product(zs):
        left_pair = split16(left_all[zs])
        for s in range(S):
            part[zs, :, pl.ds(s * rows, rows) if rows % 128 == 0 else slice(s * rows, (s + 1) * rows)] = dot3(
                left_pair, (y_high[s], y_low[s]), ((1,), (0,))
            )
        for d in range(1, T):
            scatter(zs, d).start()

    def finish(zs):
        for d in range(1, T):
            scatter(zs, d).wait_recv()
        total = part[zs, rows_of(t), :]
        for d in range(1, T):
            total = total + part_in[zs, d - 1]
        for s in range(S):
            for h in range(H):
                first = s * rows + h * width
                fin[zs, h, s] = total[:, first:first + width]
        for h in range(H):
            mine = (z * H + h == t) & (zs == z)

            @pl.when(mine)
            def _():
                out_ref[:, rows_of(t), :] = fin[zs, h]

            @pl.when(jnp.logical_not(mine))
            def _():
                final(zs, h).start()

    mix_copy = remote(mix_ref, mix_in, mix_s.at[0], mix_r.at[0], ty, z)
    mix_copy.start()
    for step in (-1, 1):
        @pl.when((z + step >= 0) & (z + step < Z))
        def _():
            psi_own(step).start()
    for c in range(CH):
        left_first(c).start()

    mix_copy.wait_recv()
    for s in range(S):
        total = mix_in[s * R, 0:1, 0:1] * right_ref[0]
        for r in range(1, R):
            total = total + mix_in[s * R + r, 0:1, 0:1] * right_ref[r]
        high, low = split16(total)
        c_high[s] = high
        c_low[s] = low

    for i in range(1, Z):
        zs = near(i)
        psi_pass(zs, 1).wait_recv()
        for step in (-1, 1):
            @pl.when(can_pass(zs, step))
            def _():
                psi_pass(zs, step).start()
        copies = spread_copies(zs)
        copies[0].start()
        copies[1].start()
        copies[3].start()

    for s in range(S):
        fill_y(z, psi_ref[s], s)

    def spread_on(zs):
        copies = spread_copies(zs)
        copies[0].wait_recv()
        copies[2].start()
        copies[4].start()
        copies[1].wait_recv()
        copies[5].start()
        copies[2].wait_recv()
        copies[6].start()

    def y_block(zs):
        copies = spread_copies(zs)
        for kind in range(3, 7):
            copies[kind].wait_recv()
        for s in range(S):
            fill_y(zs, psi_all[zs, s], s)

    left_arrives(near(0))
    for i in range(1, Z):
        spread_on(near(i))
        if i >= 2:
            y_block(near(i - 1))
            if i < Z - 1:
                left_arrives(near(i - 1))
    y_block(near(Z - 1))
    product(near(0))
    for i in range(1, Z):
        if i >= Z - 2 or i == 0:
            left_arrives(near(i))
        product(near(i))
        finish(near(i - 1))
    finish(near(Z - 1))

    for e in range(T):
        @pl.when(jnp.logical_not(own_final & (t == e)))
        def _():
            remote(
                fin.at[0, 0], out_ref.at[:, pl.ds(e * sub, sub), :],
                fin_s.at[0, 0], fin_r.at[e], t, z,
            ).wait_recv()

    mix_copy.wait_send()
    for c in range(CH):
        left_first(c).wait_send()
    for zs in range(Z):
        for step in (-1, 1):
            @pl.when(can_pass(zs, step))
            def _():
                psi_pass(zs, step).wait_send()
                for c in range(CH):
                    left_pass(zs, c, step).wait_send()

        @pl.when(zs != z)
        def _():
            for copy in spread_copies(zs):
                copy.wait_send()

        for d in range(1, T):
            scatter(zs, d).wait_send()
        for h in range(H):
            @pl.when(jnp.logical_not((z * H + h == t) & (zs == z)))
            def _():
                final(zs, h).wait_send()


def fused_device(T, Z, psi, left_ops, right_ops, term_count, right_slot, sector, sign_bit):
    S, rows, M = psi.shape
    R = right_ops.shape[0]
    H = T // Z
    sub = rows // T
    CH = 2
    weight = term_weights(right_slot, term_count, sign_bit)
    sector_hit = sector[None, :] == jnp.arange(S, dtype=jnp.int32)[:, None]
    slot_hit = right_slot[None, :] == jnp.arange(R, dtype=jnp.int32)[:, None]
    both = sector_hit[:, None, :] & slot_hit[None, :, :]
    mix = jnp.sum(jnp.where(both, weight, 0.0), axis=-1)
    mix = jnp.broadcast_to(mix.reshape(S * R, 1, 1), (S * R, 8, 128))
    dma = pltpu.SemaphoreType.DMA
    f32, b16 = jnp.float32, jnp.bfloat16
    vmem = pl.BlockSpec(memory_space=pltpu.VMEM)
    return pl.pallas_call(
        functools.partial(kernel, T, Z, CH),
        out_shape=jax.ShapeDtypeStruct((S, rows, rows // H), f32),
        in_specs=[vmem] * 4,
        out_specs=vmem,
        scratch_shapes=[
            pltpu.VMEM((Z, S, rows, M), f32),
            pltpu.VMEM((Z, rows, M), f32),
            pltpu.VMEM((S * R, 8, 128), f32),
            pltpu.VMEM((S, Z * rows, rows), b16),
            pltpu.VMEM((S, Z * rows, rows), b16),
            pltpu.VMEM((Z, rows, S * rows), f32),
            pltpu.VMEM((Z, T - 1, sub, S * rows), f32),
            pltpu.VMEM((Z, H, S, sub, rows // H), f32),
            pltpu.VMEM((S, rows, M), b16),
            pltpu.VMEM((S, rows, M), b16),
            dma((1,)), dma((1,)),
            dma((2, Z)), dma((Z,)),
            dma((Z, 7)), dma((Z, 7)),
            dma((CH,)), dma((2, Z, CH)), dma((Z, CH)),
            dma((Z, T - 1)), dma((Z, T - 1)),
            dma((Z, H)), dma((T,)),
        ],
        compiler_params=pltpu.CompilerParams(
            collective_id=0, has_side_effects=True, vmem_limit_bytes=40 * 1024 * 1024
        ),
        cost_estimate=pl.CostEstimate(
            flops=4 * S * M * M * rows, bytes_accessed=4 * 6 * rows * M, transcendentals=0
        ),
    )(psi, left_ops[0], right_ops, mix)


def solution(mesh):
    T, Z = mesh.shape["terms"], mesh.shape["rows"]

    def per_device(psi, left_ops, right_ops, *terms):
        M = psi.shape[2]
        rows = psi.shape[1]
        fits = (
            T == 8 and Z >= 4 and T % Z == 0 and M == Z * rows and M % 128 == 0
            and rows % (8 * T) == 0 and rows % 32 == 0 and left_ops.shape[0] == 1
        )
        if fits:
            return fused_device(T, Z, psi, left_ops, right_ops, *terms)
        return plain_device(psi, left_ops, right_ops, *terms)

    return jax.shard_map(
        per_device,
        mesh=mesh,
        in_specs=(
            P(None, "rows", None),
            P("terms", "rows", None),
            P("terms", "rows", None),
            P("terms"),
            P("terms"),
            P("terms"),
            P("terms"),
        ),
        out_specs=P(None, "rows", "terms"),
        check_vma=False,
    )
```

time: 276 us -> 92.1 us (0.33)
  waiting for transfers between devices: 233 us -> 0 us
  Pallas kernels: 0 us -> 85.3 us
  between operations: 13.9 us -> 0.67 us
  matrix products: 11 us -> 0 us
  loops' own time: 5.13 us -> 0 us
  local copies, waits for them, and re-layouts: 8.59 us -> 4.44 us
    all_gather x2 -> x0, waiting for transfers between devices: 144 us -> none  [the longest x1 83.9 us: per_device(): segment = lax.all_gather(moved_right, 'rows', axis=1, tiled=True)]
    pallas_call x0 -> x1, Pallas kernels: none -> 85.3 us  [fused_device(): pl.pallas_call(functools.partial(kernel, T, Z, CH), out_shape=jax.ShapeDt...]
    unnamed x4 -> x0, waiting for transfers between devices: 62.8 us -> none
    ppermute x1 -> x0, waiting for transfers between devices: 25.7 us -> none  [passed_along(): return lax.ppermute(block, axis, route)]
    dot_general x2 -> x0, matrix products: 11 us -> none  [the longest x1 5.54 us: per_device(): jnp.einsum('an,snb->sab', left_rows, lax.all_gather(psi, 'rows', axis=1,...]
    another operation x1 -> x0, loops' own time: 5.13 us -> none  [per_device(): partial_value = lax.fori_loop(0, live_count, one_term, summed_zero)]
    unnamed x18 -> x7, local copies, waits for them, and re-layouts: 6.64 us -> 4.29 us
  transfers between devices with their start and end apart: 4 -> 0, of which waited for: 4 -> 0; matrix products, arithmetic and copies ran while one was open for 2% -> 0% of each run, Pallas kernels for 0% -> 0%
where the time goes in v1:
time: 92.1 us; the launch traced here: 91.9 us
  Pallas kernels  85.3 us (93%)
  local copies, waits for them, and re-layouts  4.44 us (5%)
  other arithmetic  1.43 us (2%)
    pallas_call x1, Pallas kernels, fused_device(): pl.pallas_call(functools.partial(kernel, T, Z, CH), out_shape=jax.ShapeDt...  85.3 us
    unnamed x7, local copies, waits for them, and re-layouts  4.29 us

profile of v1, /device:TPU:25, one launch (start us, length us, event | category | flops | bytes accessed | tf_op | source)
XLA Modules:
  0.0 91.9 jit_solution(271290702426453811)
XLA Ops:
  0.7 0.7 compare_select_fusion
  1.3 0.7 iota_compare_fusion
  2.0 0.1 fusion
  2.1 0.1 broadcast_in_dim.28
  2.2 0.1 broadcast_in_dim.29.mix_ref
  2.2 0.0 copy-start
  2.2 1.3 %copy-done = f32[2,192,768]{2,1,0:T(8,128)S(1)} copy-done((f32[2,192,768]{2,1,0:T(8,128)S(1)}, f32[2,192,768]{2,1,0:T(8,128)}, u32[]{:S(2)}) %copy-start) | copy-done | bytes 1179672
  3.5 0.0 copy-start.1
  3.5 1.3 %copy-done.1 = f32[2,192,768]{2,1,0:T(8,128)S(1)} copy-done((f32[2,192,768]{2,1,0:T(8,128)S(1)}, f32[2,192,768]{2,1,0:T(8,128)}, u32[]{:S(2)}) %copy-start.1) | copy-done | bytes 1179672
  4.8 0.0 copy-start.2
  4.8 1.1 %copy-done.2 = f32[1,192,768]{2,1,0:T(8,128)S(1)} copy-done((f32[1,192,768]{2,1,0:T(8,128)S(1)}, f32[1,192,768]{2,1,0:T(8,128)}, u32[]{:S(2)}) %copy-start.2) | copy-done | bytes 589848
  5.9 85.3 %shard_map.73 = f32[2,192,96]{2,1,0:T(8,128)S(1)} custom-call(f32[2,192,768]{2,1,0:T(8,128)S(1)} %copy-done, f32[192,768]{1,0:T(8,128)S(1)} %bitcast.3, f32[2,192,768]{2,1,0:T(8,128)S(1)} %copy-done.1, f32[4,8,128]{2,1,0:T(8,128)S(1)} %broadcast_in_dim.29.mix_ref), custom_call_target="tpu_custom_call" | custom-call | flops 905969664 | bytes 3538944 | tf_op jit(solution)/shard_map/pallas_call | solution.py:331
  91.2 0.7 copy.10
Async XLA Ops:
  2.2 1.3 %copy-start = (f32[2,192,768]{2,1,0:T(8,128)S(1)}, f32[2,192,768]{2,1,0:T(8,128)}, u32[]{:S(2)}) copy-start(f32[2,192,768]{2,1,0:T(8,128)} %psi_ref.1) | copy-start | bytes 3538948
  3.5 1.3 %copy-start.1 = (f32[2,192,768]{2,1,0:T(8,128)S(1)}, f32[2,192,768]{2,1,0:T(8,128)}, u32[]{:S(2)}) copy-start(f32[2,192,768]{2,1,0:T(8,128)} %right_ref.1) | copy-start | bytes 3538948
  4.8 1.1 %copy-start.2 = (f32[1,192,768]{2,1,0:T(8,128)S(1)}, f32[1,192,768]{2,1,0:T(8,128)}, u32[]{:S(2)}) copy-start(f32[1,192,768]{2,1,0:T(8,128)} %param.8) | copy-start | bytes 1769476

commit v2 on v1

--- a/solution.py
+++ b/solution.py
@@ -69,6 +69,7 @@
     psi_ref, left_ref, right_ref, mix_ref, out_ref,
     psi_all, left_all, mix_in, y_high, y_low, part, part_in, fin,
     c_high, c_low,
+    right_in, local_s,
     mix_s, mix_r, pz_s, pz_r, pp_s, pp_r, ly_s, lz_s, l_r, sc_s, sc_r, fin_s, fin_r,
 ):
     S, rows, M = psi_ref.shape
@@ -101,6 +102,11 @@
     def rows_of(device):
         return pl.ds(pl.multiple_of(device * sub, 8), sub)
 
+    psi_copy = pltpu.make_async_copy(psi_ref, psi_all.at[z], local_s.at[0])
+    right_copy = pltpu.make_async_copy(right_ref, right_in, local_s.at[1])
+    psi_copy.start()
+    right_copy.start()
+
     barrier = pltpu.get_barrier_semaphore()
     for d in range(1, T):
         pl.semaphore_signal(barrier, 1, device_id=(lax.rem(t + d, T), z), device_id_type=MESH)
@@ -224,29 +230,34 @@
     for c in range(CH):
         left_first(c).start()
 
+    right_copy.wait()
     mix_copy.wait_recv()
     for s in range(S):
-        total = mix_in[s * R, 0:1, 0:1] * right_ref[0]
+        total = mix_in[s * R, 0:1, 0:1] * right_in[0]
         for r in range(1, R):
-            total = total + mix_in[s * R + r, 0:1, 0:1] * right_ref[r]
+            total = total + mix_in[s * R + r, 0:1, 0:1] * right_in[r]
         high, low = split16(total)
         c_high[s] = high
         c_low[s] = low
 
-    for i in range(1, Z):
-        zs = near(i)
+    def psi_arrives(zs):
         psi_pass(zs, 1).wait_recv()
         for step in (-1, 1):
             @pl.when(can_pass(zs, step))
             def _():
                 psi_pass(zs, step).start()
-        copies = spread_copies(zs)
-        copies[0].start()
-        copies[1].start()
-        copies[3].start()
-
+        spread(zs, 0, t, ty).start()
+        spread(zs, 1, t, tx).start()
+        spread(zs, 3, t, tk).start()
+
+    for i in range(1, Z - 1):
+        psi_arrives(near(i))
+    left_arrives(near(0))
+    psi_arrives(near(Z - 1))
+
+    psi_copy.wait()
     for s in range(S):
-        fill_y(z, psi_ref[s], s)
+        fill_y(z, psi_all[z, s], s)
 
     def spread_on(zs):
         copies = spread_copies(zs)
@@ -265,7 +276,6 @@
         for s in range(S):
             fill_y(zs, psi_all[zs, s], s)
 
-    left_arrives(near(0))
     for i in range(1, Z):
         spread_on(near(i))
         if i >= 2:
@@ -327,11 +337,12 @@
     mix = jnp.broadcast_to(mix.reshape(S * R, 1, 1), (S * R, 8, 128))
     dma = pltpu.SemaphoreType.DMA
     f32, b16 = jnp.float32, jnp.bfloat16
+    anyw = pl.BlockSpec(memory_space=pl.ANY)
     vmem = pl.BlockSpec(memory_space=pltpu.VMEM)
     return pl.pallas_call(
         functools.partial(kernel, T, Z, CH),
         out_shape=jax.ShapeDtypeStruct((S, rows, rows // H), f32),
-        in_specs=[vmem] * 4,
+        in_specs=[anyw] * 3 + [vmem],
         out_specs=vmem,
         scratch_shapes=[
             pltpu.VMEM((Z, S, rows, M), f32),
@@ -344,6 +355,7 @@
             pltpu.VMEM((Z, H, S, sub, rows // H), f32),
             pltpu.VMEM((S, rows, M), b16),
             pltpu.VMEM((S, rows, M), b16),
+            pltpu.VMEM((R, rows, M), f32), dma((2,)),
             dma((1,)), dma((1,)),
             dma((2, Z)), dma((Z,)),
             dma((Z, 7)), dma((Z, 7)),

time: 92.1 us -> 92.7 us (level)
  no operation moved by 1% of the time
where the time goes in v2:
time: 92.7 us; the launch traced here: 92.5 us
  Pallas kernels  85.9 us (93%)
  local copies, waits for them, and re-layouts  4.44 us (5%)
  other arithmetic  1.43 us (2%)
    pallas_call x1, Pallas kernels, fused_device(): pl.pallas_call(functools.partial(kernel, T, Z, CH), out_shape=jax.ShapeDt...  85.9 us
    unnamed x7, local copies, waits for them, and re-layouts  4.29 us

profile of v2, /device:TPU:25, one launch (start us, length us, event | category | flops | bytes accessed | tf_op | source)
XLA Modules:
  0.0 92.5 jit_solution(86183794718458788)
XLA Ops:
  0.7 0.7 compare_select_fusion
  1.3 0.7 iota_compare_fusion
  2.0 0.1 fusion
  2.1 0.1 broadcast_in_dim.28
  2.2 0.1 broadcast_in_dim.29.mix_ref
  2.2 0.0 copy-start
  2.2 1.3 %copy-done = f32[2,192,768]{2,1,0:T(8,128)S(1)} copy-done((f32[2,192,768]{2,1,0:T(8,128)S(1)}, f32[2,192,768]{2,1,0:T(8,128)}, u32[]{:S(2)}) %copy-start) | copy-done | bytes 1179672
  3.5 0.0 copy-start.1
  3.5 1.3 %copy-done.1 = f32[2,192,768]{2,1,0:T(8,128)S(1)} copy-done((f32[2,192,768]{2,1,0:T(8,128)S(1)}, f32[2,192,768]{2,1,0:T(8,128)}, u32[]{:S(2)}) %copy-start.1) | copy-done | bytes 1179672
  4.8 0.0 copy-start.2
  4.8 1.1 %copy-done.2 = f32[1,192,768]{2,1,0:T(8,128)S(1)} copy-done((f32[1,192,768]{2,1,0:T(8,128)S(1)}, f32[1,192,768]{2,1,0:T(8,128)}, u32[]{:S(2)}) %copy-start.2) | copy-done | bytes 589848
  5.9 85.9 %shard_map.73 = f32[2,192,96]{2,1,0:T(8,128)S(1)} custom-call(f32[2,192,768]{2,1,0:T(8,128)S(1)} %copy-done, f32[192,768]{1,0:T(8,128)S(1)} %bitcast.3, f32[2,192,768]{2,1,0:T(8,128)S(1)} %copy-done.1, f32[4,8,128]{2,1,0:T(8,128)S(1)} %broadcast_in_dim.29.mix_ref), custom_call_target="tpu_custom_call" | custom-call | flops 905969664 | bytes 3538944 | tf_op jit(solution)/shard_map/pallas_call | solution.py:342
  91.8 0.7 copy.10
Async XLA Ops:
  2.2 1.3 %copy-start = (f32[2,192,768]{2,1,0:T(8,128)S(1)}, f32[2,192,768]{2,1,0:T(8,128)}, u32[]{:S(2)}) copy-start(f32[2,192,768]{2,1,0:T(8,128)} %psi_ref.1) | copy-start | bytes 3538948
  3.5 1.3 %copy-start.1 = (f32[2,192,768]{2,1,0:T(8,128)S(1)}, f32[2,192,768]{2,1,0:T(8,128)}, u32[]{:S(2)}) copy-start(f32[2,192,768]{2,1,0:T(8,128)} %right_ref.1) | copy-start | bytes 3538948
  4.8 1.1 %copy-start.2 = (f32[1,192,768]{2,1,0:T(8,128)S(1)}, f32[1,192,768]{2,1,0:T(8,128)}, u32[]{:S(2)}) copy-start(f32[1,192,768]{2,1,0:T(8,128)} %param.8) | copy-start | bytes 1769476

commit v3 on v2

--- a/solution.py
+++ b/solution.py
@@ -183,13 +183,26 @@
         y_high[s, pl.ds(pl.multiple_of(zs * rows, 16), rows), :] = high
         y_low[s, pl.ds(pl.multiple_of(zs * rows, 16), rows), :] = low
 
-    def left_arrives(zs):
-        for c in range(CH):
+    is_end = (z == 0) | (z == Z - 1)
+
+    def left_arrives(zs, chunks=range(CH)):
+        for c in chunks:
             left_pass(zs, c, 1).wait_recv()
             for step in (-1, 1):
                 @pl.when(can_pass(zs, step))
                 def _():
                     left_pass(zs, c, step).start()
+
+    def inner_takes(zs):
+        @pl.when(jnp.logical_not(is_end))
+        def _():
+            left_arrives(zs)
+
+    def end_takes(zs):
+        @pl.when(is_end)
+        def _():
+            for c in range(CH):
+                left_pass(zs, c, 1).wait_recv()
 
     def product(zs):
         left_pair = split16(left_all[zs])
@@ -230,6 +243,17 @@
     for c in range(CH):
         left_first(c).start()
 
+    def psi_arrives(zs):
+        psi_pass(zs, 1).wait_recv()
+        for step in (-1, 1):
+            @pl.when(can_pass(zs, step))
+            def _():
+                psi_pass(zs, step).start()
+        spread(zs, 0, t, ty).start()
+        spread(zs, 1, t, tx).start()
+        spread(zs, 3, t, tk).start()
+
+    psi_arrives(near(1))
     right_copy.wait()
     mix_copy.wait_recv()
     for s in range(S):
@@ -239,20 +263,10 @@
         high, low = split16(total)
         c_high[s] = high
         c_low[s] = low
-
-    def psi_arrives(zs):
-        psi_pass(zs, 1).wait_recv()
-        for step in (-1, 1):
-            @pl.when(can_pass(zs, step))
-            def _():
-                psi_pass(zs, step).start()
-        spread(zs, 0, t, ty).start()
-        spread(zs, 1, t, tx).start()
-        spread(zs, 3, t, tk).start()
-
-    for i in range(1, Z - 1):
+    left_arrives(near(0), range(CH // 2))
+    for i in range(2, Z - 1):
         psi_arrives(near(i))
-    left_arrives(near(0))
+    left_arrives(near(0), range(CH // 2, CH))
     psi_arrives(near(Z - 1))
 
     psi_copy.wait()
@@ -276,17 +290,23 @@
         for s in range(S):
             fill_y(zs, psi_all[zs, s], s)
 
-    for i in range(1, Z):
+    spread_on(near(1))
+    spread_on(near(2))
+    inner_takes(near(1))
+    for i in range(3, Z):
         spread_on(near(i))
-        if i >= 2:
-            y_block(near(i - 1))
-            if i < Z - 1:
-                left_arrives(near(i - 1))
-    y_block(near(Z - 1))
+    y_block(near(1))
+    inner_takes(near(2))
+    for i in range(2, Z):
+        y_block(near(i))
     product(near(0))
-    for i in range(1, Z):
-        if i >= Z - 2 or i == 0:
-            left_arrives(near(i))
+    end_takes(near(1))
+    product(near(1))
+    for i in range(3, Z):
+        inner_takes(near(i))
+    finish(near(0))
+    for i in range(2, Z):
+        end_takes(near(i))
         product(near(i))
         finish(near(i - 1))
     finish(near(Z - 1))
@@ -328,7 +348,7 @@
     R = right_ops.shape[0]
     H = T // Z
     sub = rows // T
-    CH = 2
+    CH = 4
     weight = term_weights(right_slot, term_count, sign_bit)
     sector_hit = sector[None, :] == jnp.arange(S, dtype=jnp.int32)[:, None]
     slot_hit = right_slot[None, :] == jnp.arange(R, dtype=jnp.int32)[:, None]

time: 92.7 us -> 83.7 us (0.903)
  Pallas kernels: 85.9 us -> 76.9 us
    pallas_call x1, Pallas kernels: 85.9 us -> 76.9 us  [fused_device(): pl.pallas_call(functools.partial(kernel, T, Z, CH), out_shape=jax.ShapeDt...]
where the time goes in v3:
time: 83.7 us; the launch traced here: 83.4 us
  Pallas kernels  76.9 us (92%)
  local copies, waits for them, and re-layouts  4.44 us (5%)
  other arithmetic  1.43 us (2%)
    pallas_call x1, Pallas kernels, fused_device(): pl.pallas_call(functools.partial(kernel, T, Z, CH), out_shape=jax.ShapeDt...  76.9 us
    unnamed x7, local copies, waits for them, and re-layouts  4.29 us

profile of v3, /device:TPU:25, one launch (start us, length us, event | category | flops | bytes accessed | tf_op | source)
XLA Modules:
  0.0 83.4 jit_solution(5818031164535541548)
XLA Ops:
  0.7 0.7 compare_select_fusion
  1.3 0.7 iota_compare_fusion
  2.0 0.1 fusion
  2.1 0.1 broadcast_in_dim.28
  2.2 0.1 broadcast_in_dim.29.mix_ref
  2.2 0.0 copy-start
  2.2 1.3 %copy-done = f32[2,192,768]{2,1,0:T(8,128)S(1)} copy-done((f32[2,192,768]{2,1,0:T(8,128)S(1)}, f32[2,192,768]{2,1,0:T(8,128)}, u32[]{:S(2)}) %copy-start) | copy-done | bytes 1179672
  3.5 0.0 copy-start.1
  3.5 1.3 %copy-done.1 = f32[2,192,768]{2,1,0:T(8,128)S(1)} copy-done((f32[2,192,768]{2,1,0:T(8,128)S(1)}, f32[2,192,768]{2,1,0:T(8,128)}, u32[]{:S(2)}) %copy-start.1) | copy-done | bytes 1179672
  4.8 0.0 copy-start.2
  4.8 1.1 %copy-done.2 = f32[1,192,768]{2,1,0:T(8,128)S(1)} copy-done((f32[1,192,768]{2,1,0:T(8,128)S(1)}, f32[1,192,768]{2,1,0:T(8,128)}, u32[]{:S(2)}) %copy-start.2) | copy-done | bytes 589848
  5.9 76.9 %shard_map.73 = f32[2,192,96]{2,1,0:T(8,128)S(1)} custom-call(f32[2,192,768]{2,1,0:T(8,128)S(1)} %copy-done, f32[192,768]{1,0:T(8,128)S(1)} %bitcast.3, f32[2,192,768]{2,1,0:T(8,128)S(1)} %copy-done.1, f32[4,8,128]{2,1,0:T(8,128)S(1)} %broadcast_in_dim.29.mix_ref), custom_call_target="tpu_custom_call" | custom-call | flops 905969664 | bytes 3538944 | tf_op jit(solution)/shard_map/pallas_call | solution.py:362
  82.7 0.7 copy.10
Async XLA Ops:
  2.2 1.3 %copy-start = (f32[2,192,768]{2,1,0:T(8,128)S(1)}, f32[2,192,768]{2,1,0:T(8,128)}, u32[]{:S(2)}) copy-start(f32[2,192,768]{2,1,0:T(8,128)} %psi_ref.1) | copy-start | bytes 3538948
  3.5 1.3 %copy-start.1 = (f32[2,192,768]{2,1,0:T(8,128)S(1)}, f32[2,192,768]{2,1,0:T(8,128)}, u32[]{:S(2)}) copy-start(f32[2,192,768]{2,1,0:T(8,128)} %right_ref.1) | copy-start | bytes 3538948
  4.8 1.1 %copy-start.2 = (f32[1,192,768]{2,1,0:T(8,128)S(1)}, f32[1,192,768]{2,1,0:T(8,128)}, u32[]{:S(2)}) copy-start(f32[1,192,768]{2,1,0:T(8,128)} %param.8) | copy-start | bytes 1769476

commit v4 on v3

--- a/solution.py
+++ b/solution.py
@@ -293,11 +293,10 @@
     spread_on(near(1))
     spread_on(near(2))
     inner_takes(near(1))
+    inner_takes(near(2))
     for i in range(3, Z):
         spread_on(near(i))
-    y_block(near(1))
-    inner_takes(near(2))
-    for i in range(2, Z):
+    for i in range(1, Z):
         y_block(near(i))
     product(near(0))
     end_takes(near(1))

time: 83.7 us -> 79.5 us (0.950)
  Pallas kernels: 76.9 us -> 72.7 us
    pallas_call x1, Pallas kernels: 76.9 us -> 72.7 us  [fused_device(): pl.pallas_call(functools.partial(kernel, T, Z, CH), out_shape=jax.ShapeDt...]
where the time goes in v4:
time: 79.5 us; the launch traced here: 79.3 us
  Pallas kernels  72.7 us (91%)
  local copies, waits for them, and re-layouts  4.44 us (6%)
  other arithmetic  1.43 us (2%)
    pallas_call x1, Pallas kernels, fused_device(): pl.pallas_call(functools.partial(kernel, T, Z, CH), out_shape=jax.ShapeDt...  72.7 us
    unnamed x7, local copies, waits for them, and re-layouts  4.29 us

profile of v4, /device:TPU:25, one launch (start us, length us, event | category | flops | bytes accessed | tf_op | source)
XLA Modules:
  0.0 79.3 jit_solution(2892441308672960322)
XLA Ops:
  0.7 0.7 compare_select_fusion
  1.3 0.7 iota_compare_fusion
  2.0 0.1 fusion
  2.1 0.1 broadcast_in_dim.28
  2.2 0.1 broadcast_in_dim.29.mix_ref
  2.2 0.0 copy-start
  2.2 1.3 %copy-done = f32[2,192,768]{2,1,0:T(8,128)S(1)} copy-done((f32[2,192,768]{2,1,0:T(8,128)S(1)}, f32[2,192,768]{2,1,0:T(8,128)}, u32[]{:S(2)}) %copy-start) | copy-done | bytes 1179672
  3.5 0.0 copy-start.1
  3.5 1.3 %copy-done.1 = f32[2,192,768]{2,1,0:T(8,128)S(1)} copy-done((f32[2,192,768]{2,1,0:T(8,128)S(1)}, f32[2,192,768]{2,1,0:T(8,128)}, u32[]{:S(2)}) %copy-start.1) | copy-done | bytes 1179672
  4.8 0.0 copy-start.2
  4.8 1.1 %copy-done.2 = f32[1,192,768]{2,1,0:T(8,128)S(1)} copy-done((f32[1,192,768]{2,1,0:T(8,128)S(1)}, f32[1,192,768]{2,1,0:T(8,128)}, u32[]{:S(2)}) %copy-start.2) | copy-done | bytes 589848
  5.9 72.7 %shard_map.73 = f32[2,192,96]{2,1,0:T(8,128)S(1)} custom-call(f32[2,192,768]{2,1,0:T(8,128)S(1)} %copy-done, f32[192,768]{1,0:T(8,128)S(1)} %bitcast.3, f32[2,192,768]{2,1,0:T(8,128)S(1)} %copy-done.1, f32[4,8,128]{2,1,0:T(8,128)S(1)} %broadcast_in_dim.29.mix_ref), custom_call_target="tpu_custom_call" | custom-call | flops 905969664 | bytes 3538944 | tf_op jit(solution)/shard_map/pallas_call | solution.py:361
  78.6 0.7 copy.10
Async XLA Ops:
  2.2 1.3 %copy-start = (f32[2,192,768]{2,1,0:T(8,128)S(1)}, f32[2,192,768]{2,1,0:T(8,128)}, u32[]{:S(2)}) copy-start(f32[2,192,768]{2,1,0:T(8,128)} %psi_ref.1) | copy-start | bytes 3538948
  3.5 1.3 %copy-start.1 = (f32[2,192,768]{2,1,0:T(8,128)S(1)}, f32[2,192,768]{2,1,0:T(8,128)}, u32[]{:S(2)}) copy-start(f32[2,192,768]{2,1,0:T(8,128)} %right_ref.1) | copy-start | bytes 3538948
  4.8 1.1 %copy-start.2 = (f32[1,192,768]{2,1,0:T(8,128)S(1)}, f32[1,192,768]{2,1,0:T(8,128)}, u32[]{:S(2)}) copy-start(f32[1,192,768]{2,1,0:T(8,128)} %param.8) | copy-start | bytes 1769476
